TPU v7x, 32 devices: a whole 2x2x4 slice. The times are simulated.
32 devices in a mesh: blk: 8 (over y, x, core), group: 4 (over z).
Axes of the slice: x: 2, y: 2, z: 4, core: 2. Of those that a mesh axis runs over, the one named last changes fastest.
Arguments:
- visual_encoder_outputs: float32 [16384, 1152], P(('blk', 'group'))
- caption_encoder_outputs: float32 [16384, 1152], P(('blk', 'group'))
- partner_lookup_grid: int32 [2, 8], replicated, may hold values from 0 to 7, as said below
- sharpness_coefficient: float32 [1], replicated, may hold values from 8 to 30
- sigmoid_shift_term: float32 [1], replicated, may hold values from -6 to -2
Outputs:
- image_gradient: float32 [16384, 1152], P(('blk', 'group'))
- text_gradient: float32 [16384, 1152], P(('blk', 'group'))
Inputs may be any that keep to these rules, and one draw needn't show every extreme that they name: In each of the 2 rounds, partner_lookup_grid pairs index b of blk with index b XOR 2**k, where k is a bit position drawn for that round; the rounds' positions differ, so every matching is mutual and no index meets the same partner twice.
All inputs are finite; a program needn't handle non-finite values.
Results may differ from a plain program's by a relative error of at most 0.0049.
Values may be sent and summed in bfloat16 or wider, within the bound.
No kernel may reach another device: no remote copies, remote signals or barrier semaphores. Data moves between devices by JAX's collectives and lax.ppermute only.
A program may use at most 64 MiB of HBM per device.

v0:
```python
import functools
import itertools

import jax
import jax.numpy as jnp
from jax import lax
from jax.experimental import pallas as pl
from jax.experimental.pallas import tpu as pltpu
from jax.sharding import PartitionSpec as P

epsilon = 1e-06
MIB = 1024 * 1024
VMEM = pl.BlockSpec(memory_space=pltpu.VMEM)
SMEM = pl.BlockSpec(memory_space=pltpu.SMEM)
ANY = pl.BlockSpec(memory_space=pl.ANY)


def radius_of(raw):
    return jnp.sqrt(jnp.sum(raw * raw, axis=-1, keepdims=True) + epsilon)


def halves_kernel(raw_ref, half_ref):
    raw = raw_ref[...]
    half_ref[...] = (raw / radius_of(raw)).astype(jnp.bfloat16)


def halves(raw, blocks=4):
    rows, width = raw.shape
    spec = pl.BlockSpec((rows // blocks, width), lambda i: (i, 0))
    return pl.pallas_call(
        halves_kernel,
        grid=(blocks,),
        in_specs=[spec],
        out_specs=spec,
        out_shape=jax.ShapeDtypeStruct((rows, width), jnp.bfloat16),
        name="halves",
        cost_estimate=pl.CostEstimate(flops=4 * rows * width, bytes_accessed=6 * rows * width, transcendentals=rows),
    )(raw)


def add_up_kernel(matched, has_sum, has_raw, scale_ref, shift_ref, own_ref, *refs):
    refs = list(refs)
    other_refs = [refs.pop(0) for _ in matched]
    sum_ref = refs.pop(0) if has_sum else None
    raw_ref = refs.pop(0) if has_raw else None
    out_ref = refs.pop(0)
    block = own_ref.shape[0]
    scale, shift = scale_ref[0], shift_ref[0]
    own = own_ref[...]
    total = sum_ref[...] if has_sum else None
    for other_ref, is_matched in zip(other_refs, matched):
        other = other_ref[...]
        products = lax.dot_general(
            own, other, (((1,), (1,)), ((), ())), preferred_element_type=jnp.float32
        )
        logits = scale * products + shift
        if is_matched:
            row = pl.program_id(0) * block + lax.broadcasted_iota(jnp.int32, logits.shape, 0)
            column = lax.broadcasted_iota(jnp.int32, logits.shape, 1)
            same = row == column
            weights = scale / (1.0 + jnp.exp(jnp.where(same, logits, -logits)))
            weights = jnp.where(same, -weights, weights)
        else:
            weights = scale / (1.0 + jnp.exp(-logits))
        added = jnp.dot(weights.astype(jnp.bfloat16), other, preferred_element_type=jnp.float32)
        total = added if total is None else total + added
    if has_raw:
        raw = raw_ref[...]
        radius = radius_of(raw)
        unit = raw / radius
        radial = jnp.sum(unit * total, axis=-1, keepdims=True)
        total = (total - unit * radial) / radius
    out_ref[...] = total


def add_up(scale, shift, own, others, matched, total=None, raw=None, blocks=2):
    rows, width = own.shape
    spec = pl.BlockSpec((rows // blocks, width), lambda i: (i, 0))
    whole = VMEM
    operands = [own, *others] + [x for x in (total, raw) if x is not None]
    specs = [spec] + [whole] * len(others) + [spec] * (len(operands) - 1 - len(others))
    other_rows = sum(x.shape[0] for x in others)
    return pl.pallas_call(
        functools.partial(add_up_kernel, tuple(matched), total is not None, raw is not None),
        grid=(blocks,),
        in_specs=[SMEM, SMEM] + specs,
        out_specs=spec,
        out_shape=jax.ShapeDtypeStruct((rows, width), jnp.float32),
        name="add_up",
        compiler_params=pltpu.CompilerParams(vmem_limit_bytes=32 * MIB),
        cost_estimate=pl.CostEstimate(
            flops=4 * rows * other_rows * width,
            bytes_accessed=sum(x.size * x.dtype.itemsize for x in operands) + 4 * rows * width,
            transcendentals=2 * rows * other_rows,
        ),
    )(scale, shift, *operands)


def passed_along(x, axis, by):
    count = lax.axis_size(axis)
    return lax.ppermute(x, axis, [(i, (i + by) % count) for i in range(count)])


def exchanged(x, bit):
    count = lax.axis_size("blk")
    return lax.ppermute(x, "blk", [(i, i ^ (1 << bit)) for i in range(count)])


def with_partners(bits, visual, caption, text_half, scale, shift):
    add = functools.partial(add_up, scale, shift)
    other_texts = [passed_along(text_half, "group", 1)]
    other_texts += [exchanged(text_half, bit) for bit in reversed(bits)]
    image_half = halves(visual)
    other_images = [passed_along(image_half, "group", -1)]
    other_images += [exchanged(image_half, bit) for bit in reversed(bits)]
    image_sum = add(image_half, [text_half], [True])
    text_sum = add(text_half, [image_half], [True])
    text_z, *text_p = other_texts
    image_z, *image_p = other_images
    image_gradient = add(image_half, other_texts, [False] * 3, image_sum, visual)
    text_gradient = add(text_half, other_images, [False] * 3, text_sum, caption)
    return image_gradient, text_gradient


def on_device(
    visual_encoder_outputs,
    caption_encoder_outputs,
    partner_lookup_grid,
    sharpness_coefficient,
    sigmoid_shift_term,
):
    rounds, peers = partner_lookup_grid.shape
    choices = list(itertools.combinations(range(peers.bit_length() - 1), rounds))
    union = jnp.sum(partner_lookup_grid[:, 0])
    branch = jnp.int32(0)
    for number, bits in enumerate(choices):
        branch = jnp.where(union == sum(1 << bit for bit in bits), jnp.int32(number), branch)
    text_half = halves(caption_encoder_outputs)
    return lax.switch(
        branch,
        [functools.partial(with_partners, bits) for bits in choices],
        visual_encoder_outputs,
        caption_encoder_outputs,
        text_half,
        sharpness_coefficient,
        sigmoid_shift_term,
    )


def solution(mesh):
    placed = (P(("blk", "group"), None), P(("blk", "group"), None), P(), P(), P())
    return jax.shard_map(
        on_device,
        mesh=mesh,
        in_specs=placed,
        out_specs=(P(("blk", "group"), None), P(("blk", "group"), None)),
        check_vma=False,
    )
```

profile of v0, /device:TPU:16, one launch (start us, length us, event | category | flops | bytes accessed | tf_op | source)
XLA Modules:
  0.0 90.6 jit_solution(5941935593453173159)
XLA Ops:
  0.6 1.3 %slice_reduce_fusion = s32[]{:T(128)} fusion(s32[2,8]{1,0:T(2,128)} %param.10), kind=kLoop, calls=%fused_computation | loop fusion | flops 1 | bytes 12 | tf_op jit(solution)/shard_map/reduce_sum | solution.py:134
  3.3 3.9 %halves.7 = bf16[512,1152]{1,0:T(8,128)(2,1)} custom-call(f32[512,1152]{1,0:T(8,128)} %raw_ref.1), custom_call_target="tpu_custom_call" | custom-call | flops 2359296 | bytes 3538944 | tf_op jit(solution)/shard_map/halves/pallas_call | solution.py:30
  7.2 83.4 %conditional.1 = (f32[512,1152]{1,0:T(8,128)}, f32[512,1152]{1,0:T(8,128)}) conditional(s32[]{:T(128)} %clamp.3, (f32[512,1152]{1,0:T(8,128)}, bf16[512,1152]{1,0:T(8,128)(2,1)}, f32[1]{0:T(128)}, f32[1]{0:T(128)}, f32[512,1152]{1,0:T(8,128)}) %tuple.19, (f32[512,1152]{1,0:T(8,128)}, bf16[512,1152]{1,0:T(8,128)(2,1)}, f32[1]{0:T(128)}, ...), branch_computations={%region_1.2_spmd, %region_2.3_spmd, %region_3.4_spmd} | conditional | flops 9666035712 | bytes 93192552 | solution.py:139
  7.2 1.6 %collective-permute-start.12 = (bf16[512,1152]{1,0:T(8,128)(2,1)}, bf16[512,1152]{1,0:T(8,128)(2,1)S(1)}, u32[]{:S(2)}, u32[]{:S(2)}) collective-permute-start(bf16[512,1152]{1,0:T(8,128)(2,1)} %get-tuple-element.43.refs_0_.own_ref), channel_id=1, source_target_pairs={{0,1},{1,2},{2,3},{3,0},{4,5},{5,6},{6,7},{7,4},{8,9},{9,10},{10,1... | collective-permute-start | bytes 3538952 | tf_op jit(solution)/shard_map/cond/branch_2_fun/ppermute | solution.py:101
  8.8 1.5 %collective-permute-start.13 = (bf16[512,1152]{1,0:T(8,128)(2,1)}, bf16[512,1152]{1,0:T(8,128)(2,1)S(1)}, u32[]{:S(2)}, u32[]{:S(2)}) collective-permute-start(bf16[512,1152]{1,0:T(8,128)(2,1)} %get-tuple-element.43.refs_0_.own_ref), channel_id=1, source_target_pairs={{0,16},{4,20},{8,24},{12,28},{16,0},{20,4},{24,8},{28,12},{1,17},{... | collective-permute-start | bytes 3538952 | tf_op jit(solution)/shard_map/cond/branch_2_fun/ppermute | solution.py:106
  10.3 1.5 %collective-permute-start.14 = (bf16[512,1152]{1,0:T(8,128)(2,1)}, bf16[512,1152]{1,0:T(8,128)(2,1)S(1)}, u32[]{:S(2)}, u32[]{:S(2)}) collective-permute-start(bf16[512,1152]{1,0:T(8,128)(2,1)} %get-tuple-element.43.refs_0_.own_ref), channel_id=1, source_target_pairs={{0,8},{4,12},{8,0},{12,4},{16,24},{20,28},{24,16},{28,20},{1,9},{5... | collective-permute-start | bytes 3538952 | tf_op jit(solution)/shard_map/cond/branch_2_fun/ppermute | solution.py:106
  11.8 3.9 %halves.6.own_ref.refs_0_ = bf16[512,1152]{1,0:T(8,128)(2,1)} custom-call(f32[512,1152]{1,0:T(8,128)} %get-tuple-element.60.raw_ref.refs_4_), custom_call_target="tpu_custom_call" | custom-call | flops 2359296 | bytes 3538944 | tf_op jit(solution)/shard_map/cond/branch_2_fun/halves/pallas_call | solution.py:30
  15.7 0.4 collective-permute-start.15
  16.1 0.5 collective-permute-start.16
  16.6 43.7 %collective-permute-done.12.refs_0_ = bf16[512,1152]{1,0:T(8,128)(2,1)S(1)} collective-permute-done((bf16[512,1152]{1,0:T(8,128)(2,1)}, bf16[512,1152]{1,0:T(8,128)(2,1)S(1)}, u32[]{:S(2)}, u32[]{:S(2)}) %collective-permute-start.12) | collective-permute-done | bytes 1179680 | tf_op jit(solution)/shard_map/cond/branch_2_fun/ppermute | solution.py:101
  60.4 1.5 %collective-permute-start.17 = (bf16[512,1152]{1,0:T(8,128)(2,1)}, bf16[512,1152]{1,0:T(8,128)(2,1)S(1)}, u32[]{:S(2)}, u32[]{:S(2)}) collective-permute-start(bf16[512,1152]{1,0:T(8,128)(2,1)} %halves.6.own_ref.refs_0_), channel_id=1, source_target_pairs={{0,8},{4,12},{8,0},{12,4},{16,24},{20,28},{24,16},{28,20},{1,9},{5... | collective-permute-start | bytes 3538952 | tf_op jit(solution)/shard_map/cond/branch_2_fun/ppermute | solution.py:106
  61.9 1.3 %copy-done.4 = bf16[512,1152]{1,0:T(8,128)(2,1)S(1)} copy-done((bf16[512,1152]{1,0:T(8,128)(2,1)S(1)}, bf16[512,1152]{1,0:T(8,128)(2,1)}, u32[]{:S(2)}) %copy-start.4) | copy-done | bytes 1179672 | tf_op jit(solution)/shard_map/cond
  63.2 4.8 %add_up.20.refs_3_ = f32[512,1152]{1,0:T(8,128)S(1)} custom-call(f32[1]{0:T(128)} %get-tuple-element.63.scale_ref, f32[1]{0:T(128)} %get-tuple-element.66.shift_ref, bf16[512,1152]{1,0:T(8,128)(2,1)S(1)} %copy-done.4, bf16[512,1152]{1,0:T(8,128)(2,1)} %get-tuple-element.43.refs_0_.own_ref), custom_call_target="tpu_custom_call" | custom-call | flops 1207959552 | bytes 4718592 | tf_op jit(solution)/shard_map/cond/branch_2_fun/add_up/pallas_call | solution.py:83
  68.0 0.0 copy-start.5
  68.0 0.0 copy-start.8
  68.0 5.0 %add_up.22.refs_3_ = f32[512,1152]{1,0:T(8,128)S(1)} custom-call(f32[1]{0:T(128)} %get-tuple-element.63.scale_ref, f32[1]{0:T(128)} %get-tuple-element.66.shift_ref, bf16[512,1152]{1,0:T(8,128)(2,1)} %get-tuple-element.43.refs_0_.own_ref, bf16[512,1152]{1,0:T(8,128)(2,1)S(1)} %copy-done.4), custom_call_target="tpu_custom_call" | custom-call | flops 1207959552 | bytes 4718592 | tf_op jit(solution)/shard_map/cond/branch_2_fun/add_up/pallas_call | solution.py:83
  73.1 0.0 copy-start.11
  73.1 0.0 collective-permute-done.13.refs_1_
  73.1 0.0 collective-permute-done.14.refs_2_
  73.1 8.3 %add_up.21 = f32[512,1152]{1,0:T(8,128)} custom-call(f32[1]{0:T(128)} %get-tuple-element.63.scale_ref, f32[1]{0:T(128)} %get-tuple-element.66.shift_ref, bf16[512,1152]{1,0:T(8,128)(2,1)S(1)} %copy-done.5, bf16[512,1152]{1,0:T(8,128)(2,1)S(1)} %collective-permute-done.12.refs_0_, bf16[512,1152]{1,0:T(8,128)(2,1)S(1)} %collective-permute-done.13.refs_1_, ...), custom_call_target="tpu_custom_call" | custom-call | flops 3623878656 | bytes 11796480 | tf_op jit(solution)/shard_map/cond/branch_2_fun/add_up/pallas_call | solution.py:83
  81.4 0.0 collective-permute-done.15.refs_0_
  81.4 0.0 collective-permute-done.16.refs_1_
  81.4 0.0 collective-permute-done.17.refs_2_
  81.4 9.2 %add_up.23 = f32[512,1152]{1,0:T(8,128)} custom-call(f32[1]{0:T(128)} %get-tuple-element.63.scale_ref, f32[1]{0:T(128)} %get-tuple-element.66.shift_ref, bf16[512,1152]{1,0:T(8,128)(2,1)} %get-tuple-element.43.refs_0_.own_ref, bf16[512,1152]{1,0:T(8,128)(2,1)S(1)} %collective-permute-done.15.refs_0_, bf16[512,1152]{1,0:T(8,128)(2,1)S(1)} %collective-permute-done.16.refs_1_, ...), custom_call_target="tpu_custom_call" | custom-call | flops 3623878656 | bytes 11796480 | tf_op jit(solution)/shard_map/cond/branch_2_fun/add_up/pallas_call | solution.py:83
  (4 shorter events, 0.0 us)
Async XLA Ops:
  7.2 53.2 %collective-permute-start.12 = (bf16[512,1152]{1,0:T(8,128)(2,1)}, bf16[512,1152]{1,0:T(8,128)(2,1)S(1)}, u32[]{:S(2)}, u32[]{:S(2)}) collective-permute-start(bf16[512,1152]{1,0:T(8,128)(2,1)} %get-tuple-element.43.refs_0_.own_ref), channel_id=1, source_target_pairs={{0,1},{1,2},{2,3},{3,0},{4,5},{5,6},{6,7},{7,4},{8,9},{9,10},{10,1... | collective-permute-start | bytes 3538952 | tf_op jit(solution)/shard_map/cond/branch_2_fun/ppermute | solution.py:101
  8.8 64.3 %collective-permute-start.13 = (bf16[512,1152]{1,0:T(8,128)(2,1)}, bf16[512,1152]{1,0:T(8,128)(2,1)S(1)}, u32[]{:S(2)}, u32[]{:S(2)}) collective-permute-start(bf16[512,1152]{1,0:T(8,128)(2,1)} %get-tuple-element.43.refs_0_.own_ref), channel_id=1, source_target_pairs={{0,16},{4,20},{8,24},{12,28},{16,0},{20,4},{24,8},{28,12},{1,17},{... | collective-permute-start | bytes 3538952 | tf_op jit(solution)/shard_map/cond/branch_2_fun/ppermute | solution.py:106
  10.3 62.8 %collective-permute-start.14 = (bf16[512,1152]{1,0:T(8,128)(2,1)}, bf16[512,1152]{1,0:T(8,128)(2,1)S(1)}, u32[]{:S(2)}, u32[]{:S(2)}) collective-permute-start(bf16[512,1152]{1,0:T(8,128)(2,1)} %get-tuple-element.43.refs_0_.own_ref), channel_id=1, source_target_pairs={{0,8},{4,12},{8,0},{12,4},{16,24},{20,28},{24,16},{28,20},{1,9},{5... | collective-permute-start | bytes 3538952 | tf_op jit(solution)/shard_map/cond/branch_2_fun/ppermute | solution.py:106
  15.7 65.7 %collective-permute-start.15 = (bf16[512,1152]{1,0:T(8,128)(2,1)}, bf16[512,1152]{1,0:T(8,128)(2,1)S(1)}, u32[]{:S(2)}, u32[]{:S(2)}) collective-permute-start(bf16[512,1152]{1,0:T(8,128)(2,1)} %halves.6.own_ref.refs_0_), channel_id=1, source_target_pairs={{0,3},{1,0},{2,1},{3,2},{4,7},{5,4},{6,5},{7,6},{8,11},{9,8},{10,9... | collective-permute-start | bytes 3538952 | tf_op jit(solution)/shard_map/cond/branch_2_fun/ppermute | solution.py:101
  16.1 65.3 %collective-permute-start.16 = (bf16[512,1152]{1,0:T(8,128)(2,1)}, bf16[512,1152]{1,0:T(8,128)(2,1)S(1)}, u32[]{:S(2)}, u32[]{:S(2)}) collective-permute-start(bf16[512,1152]{1,0:T(8,128)(2,1)} %halves.6.own_ref.refs_0_), channel_id=1, source_target_pairs={{0,16},{4,20},{8,24},{12,28},{16,0},{20,4},{24,8},{28,12},{1,17},{... | collective-permute-start | bytes 3538952 | tf_op jit(solution)/shard_map/cond/branch_2_fun/ppermute | solution.py:106
  60.4 21.0 %collective-permute-start.17 = (bf16[512,1152]{1,0:T(8,128)(2,1)}, bf16[512,1152]{1,0:T(8,128)(2,1)S(1)}, u32[]{:S(2)}, u32[]{:S(2)}) collective-permute-start(bf16[512,1152]{1,0:T(8,128)(2,1)} %halves.6.own_ref.refs_0_), channel_id=1, source_target_pairs={{0,8},{4,12},{8,0},{12,4},{16,24},{20,28},{24,16},{28,20},{1,9},{5... | collective-permute-start | bytes 3538952 | tf_op jit(solution)/shard_map/cond/branch_2_fun/ppermute | solution.py:106
  61.9 1.3 %copy-start.4 = (bf16[512,1152]{1,0:T(8,128)(2,1)S(1)}, bf16[512,1152]{1,0:T(8,128)(2,1)}, u32[]{:S(2)}) copy-start(bf16[512,1152]{1,0:T(8,128)(2,1)} %halves.6.own_ref.refs_0_) | copy-start | bytes 3538948 | tf_op jit(solution)/shard_map/cond
  68.0 5.1 %copy-start.5 = (bf16[512,1152]{1,0:T(8,128)(2,1)S(1)}, bf16[512,1152]{1,0:T(8,128)(2,1)}, u32[]{:S(2)}) copy-start(bf16[512,1152]{1,0:T(8,128)(2,1)} %halves.6.own_ref.refs_0_) | copy-start | bytes 3538948 | tf_op jit(solution)/shard_map/cond
  68.0 5.1 %copy-start.8 = (f32[512,1152]{1,0:T(8,128)S(1)}, f32[512,1152]{1,0:T(8,128)}, u32[]{:S(2)}) copy-start(f32[512,1152]{1,0:T(8,128)} %get-tuple-element.60.raw_ref.refs_4_) | copy-start | bytes 7077892 | tf_op jit(solution)/shard_map/cond
  73.1 8.4 %copy-start.11 = (f32[512,1152]{1,0:T(8,128)S(1)}, f32[512,1152]{1,0:T(8,128)}, u32[]{:S(2)}) copy-start(f32[512,1152]{1,0:T(8,128)} %get-tuple-element.44.refs_4_) | copy-start | bytes 7077892 | tf_op jit(solution)/shard_map/cond
where the time goes:
time: 90.7 us; the launch traced here: 90.6 us
  waiting for transfers between devices  43.8 us (48%)
  Pallas kernels  35.2 us (39%)
  starting transfers between devices  7.03 us (8%)
  between operations  1.94 us (2%)
  other arithmetic  1.32 us (1%)
  local copies, waits for them, and re-layouts  1.32 us (1%)
    ppermute x2, waiting for transfers between devices, passed_along(): return lax.ppermute(x, axis, [(i, (i + by) % count) for i in range(count)])  43.8 us
    pallas_call x4, Pallas kernels, add_up(): pl.pallas_call(functools.partial(add_up_kernel, tuple(matched), total is...  27.3 us
    pallas_call x2, Pallas kernels, halves(): pl.pallas_call(halves_kernel, grid=(blocks,), in_specs=[spec], out_specs=...  7.84 us
    ppermute x4, starting transfers between devices, exchanged(): return lax.ppermute(x, 'blk', [(i, i ^ 1 << bit) for i in range(count)])  5.01 us
    ppermute x2, starting transfers between devices, passed_along(): return lax.ppermute(x, axis, [(i, (i + by) % count) for i in range(count)])  2.03 us
  transfers between devices with their start and end apart: 6, of which 1 were waited for; matrix products, arithmetic and copies ran while one was open for 0% of the time, Pallas kernels for 24%

commit v1 on v0

v1 whole, which is shorter than its diff:
```python
import functools
import itertools

import jax
import jax.numpy as jnp
from jax import lax
from jax.experimental import pallas as pl
from jax.experimental.pallas import tpu as pltpu
from jax.sharding import PartitionSpec as P

epsilon = 1e-06
log2_e = 1.4426950408889634
MIB = 1024 * 1024
VMEM = pl.BlockSpec(memory_space=pltpu.VMEM)
SMEM = pl.BlockSpec(memory_space=pltpu.SMEM)


def inverse_radius(raw):
    return lax.rsqrt(jnp.sum(raw * raw, axis=-1, keepdims=True) + epsilon)


def halves_kernel(raw_ref, half_ref):
    raw = raw_ref[...]
    half_ref[...] = (raw * inverse_radius(raw)).astype(jnp.bfloat16)


def halves(raw, blocks=4):
    rows, width = raw.shape
    spec = pl.BlockSpec((rows // blocks, width), lambda i: (i, 0))
    return pl.pallas_call(
        halves_kernel,
        grid=(blocks,),
        in_specs=[spec],
        out_specs=spec,
        out_shape=jax.ShapeDtypeStruct((rows, width), jnp.bfloat16),
        name="halves",
        cost_estimate=cost([raw], rows, width, 0),
    )(raw)


def choosing_kernel(unions, grid_ref, raw_ref, half_ref, branch_ref):
    halves_kernel(raw_ref, half_ref)
    union = grid_ref[0, 0]
    for number in range(1, grid_ref.shape[0]):
        union = union + grid_ref[number, 0]
    branch = jnp.int32(0)
    for number, each in enumerate(unions):
        branch = jnp.where(union == each, jnp.int32(number), branch)
    branch_ref[0] = branch


def halves_and_branch(raw, grid, unions, blocks=4):
    rows, width = raw.shape
    spec = pl.BlockSpec((rows // blocks, width), lambda i: (i, 0))
    return pl.pallas_call(
        functools.partial(choosing_kernel, unions),
        grid=(blocks,),
        in_specs=[SMEM, spec],
        out_specs=[spec, SMEM],
        out_shape=[
            jax.ShapeDtypeStruct((rows, width), jnp.bfloat16),
            jax.ShapeDtypeStruct((1,), jnp.int32),
        ],
        name="halves_and_branch",
        cost_estimate=cost([raw], rows, width, 0),
    )(grid, raw)


def coupling(own, other, scale, shift, first_row=None):
    products = lax.dot_general(
        own, other, (((1,), (1,)), ((), ())), preferred_element_type=jnp.float32
    )
    powers = products * (-log2_e * scale) - log2_e * shift
    if first_row is None:
        return (scale / (1.0 + jnp.exp2(powers))).astype(jnp.bfloat16)
    row = first_row + lax.broadcasted_iota(jnp.int32, powers.shape, 0)
    same = row == lax.broadcasted_iota(jnp.int32, powers.shape, 1)
    weights = scale / (1.0 + jnp.exp2(jnp.where(same, -powers, powers)))
    return jnp.where(same, -weights, weights).astype(jnp.bfloat16)


def add_up_kernel(matched, has_sum, blocks, scale_ref, shift_ref, own_ref, *refs):
    refs = list(refs)
    other_refs = [refs.pop(0) for _ in matched]
    sum_ref = refs.pop(0) if has_sum else None
    out_ref = refs.pop(0)
    block = own_ref.shape[0] // blocks
    scale, shift = scale_ref[0], shift_ref[0]
    for number in range(blocks):
        rows = pl.ds(number * block, block)
        own = own_ref[rows, :]
        total = sum_ref[rows, :] if has_sum else None
        for other_ref, is_matched in zip(other_refs, matched):
            other = other_ref[...]
            weights = coupling(own, other, scale, shift, number * block if is_matched else None)
            added = jnp.dot(weights, other, preferred_element_type=jnp.float32)
            total = added if total is None else total + added
        out_ref[rows, :] = total


def finish_kernel(has_sum, scale_ref, shift_ref, own_ref, raw_ref, *refs):
    refs = list(refs)
    out_ref = refs.pop()
    sum_ref = refs.pop() if has_sum else None
    block = out_ref.shape[0]
    rows = pl.ds(pl.multiple_of(pl.program_id(0) * block, block), block)
    scale, shift = scale_ref[0], shift_ref[0]
    own = own_ref[rows, :]
    raw = raw_ref[rows, :]
    total = sum_ref[rows, :] if has_sum else None
    for other_ref in refs:
        other = other_ref[...]
        weights = coupling(own, other, scale, shift)
        added = jnp.dot(weights, other, preferred_element_type=jnp.float32)
        total = added if total is None else total + added
    inverse = inverse_radius(raw)
    unit = raw * inverse
    radial = jnp.sum(unit * total, axis=-1, keepdims=True)
    out_ref[...] = (total - unit * radial) * inverse


def cost(operands, rows, width, other_rows):
    return pl.CostEstimate(
        flops=4 * rows * other_rows * width,
        bytes_accessed=sum(x.size * x.dtype.itemsize for x in operands) + 4 * rows * width,
        transcendentals=2 * rows * other_rows,
    )


def add_up(scale, shift, own, others, total=None, matched=False, blocks=1):
    rows, width = own.shape
    operands = [own, *others] + ([] if total is None else [total])
    return pl.pallas_call(
        functools.partial(
            add_up_kernel, (matched,) * len(others), total is not None, blocks
        ),
        in_specs=[SMEM, SMEM] + [VMEM] * len(operands),
        out_specs=VMEM,
        out_shape=jax.ShapeDtypeStruct((rows, width), jnp.float32),
        name="add_up",
        compiler_params=pltpu.CompilerParams(vmem_limit_bytes=24 * MIB),
        cost_estimate=cost(operands, rows, width, sum(x.shape[0] for x in others)),
    )(scale, shift, *operands)


def finish(scale, shift, own, raw, others, total, blocks=2):
    rows, width = own.shape
    operands = [own, raw, *others] + ([] if total is None else [total])
    return pl.pallas_call(
        functools.partial(finish_kernel, total is not None),
        grid=(blocks,),
        in_specs=[SMEM, SMEM] + [VMEM] * len(operands),
        out_specs=pl.BlockSpec((rows // blocks, width), lambda i: (i, 0)),
        out_shape=jax.ShapeDtypeStruct((rows, width), jnp.float32),
        name="finish",
        compiler_params=pltpu.CompilerParams(vmem_limit_bytes=24 * MIB),
        cost_estimate=cost(operands, rows, width, sum(x.shape[0] for x in others)),
    )(scale, shift, *operands)


def passed_along(x, axis, by):
    count = lax.axis_size(axis)
    return lax.ppermute(x, axis, [(i, (i + by) % count) for i in range(count)])


def exchanged(x, bit):
    count = lax.axis_size("blk")
    return lax.ppermute(x, "blk", [(i, i ^ (1 << bit)) for i in range(count)])


def with_partners(bits, visual, caption, text_half, scale, shift):
    texts = [exchanged(text_half, bit) for bit in bits]
    texts += [passed_along(text_half, "group", 1)]
    image_half = halves(visual)
    image_sum = add_up(scale, shift, image_half, [text_half], matched=True)
    text_sum = add_up(scale, shift, text_half, [image_half], matched=True)
    image_half, texts, image_sum, text_sum = lax.optimization_barrier(
        (image_half, texts, image_sum, text_sum)
    )
    images = [exchanged(image_half, bit) for bit in bits]
    images += [passed_along(image_half, "group", -1)]
    image_gradient = finish(scale, shift, image_half, visual, texts, image_sum)
    text_gradient = finish(scale, shift, text_half, caption, images, text_sum)
    return image_gradient, text_gradient


def on_device(
    visual_encoder_outputs,
    caption_encoder_outputs,
    partner_lookup_grid,
    sharpness_coefficient,
    sigmoid_shift_term,
):
    rounds, peers = partner_lookup_grid.shape
    choices = list(itertools.combinations(range(peers.bit_length() - 1), rounds))
    unions = [sum(1 << bit for bit in bits) for bits in choices]
    text_half, branch = halves_and_branch(caption_encoder_outputs, partner_lookup_grid, unions)
    return lax.switch(
        branch[0],
        [functools.partial(with_partners, bits) for bits in choices],
        visual_encoder_outputs,
        caption_encoder_outputs,
        text_half,
        sharpness_coefficient,
        sigmoid_shift_term,
    )


def solution(mesh):
    placed = (P(("blk", "group"), None), P(("blk", "group"), None), P(), P(), P())
    return jax.shard_map(
        on_device,
        mesh=mesh,
        in_specs=placed,
        out_specs=(P(("blk", "group"), None), P(("blk", "group"), None)),
        check_vma=False,
    )
```

time: 90.7 us -> 74.8 us (0.82)
  the two profiles are of different devices: /device:TPU:16 before, /device:TPU:0 now
where the time goes in v1:
time: 74.8 us; the launch traced here: 74.4 us
  Pallas kernels  34.2 us (46%)
  waiting for transfers between devices  29.6 us (40%)
  starting transfers between devices  7.94 us (11%)
  local copies, waits for them, and re-layouts  1.28 us (2%)
  between operations  1.28 us (2%)
    ppermute x2, waiting for transfers between devices, passed_along(): return lax.ppermute(x, axis, [(i, (i + by) % count) for i in range(count)])  28.4 us
    pallas_call x2, Pallas kernels, finish(): pl.pallas_call(functools.partial(finish_kernel, total is not None), grid=...  17.7 us
    pallas_call x2, Pallas kernels, add_up(): pl.pallas_call(functools.partial(add_up_kernel, (matched,) * len(others),...  8.68 us
    ppermute x2, starting transfers between devices, passed_along(): return lax.ppermute(x, axis, [(i, (i + by) % count) for i in range(count)])  4.89 us
    pallas_call x1, Pallas kernels, halves_and_branch(): pl.pallas_call(functools.partial(choosing_kernel, unions), grid=(blocks,)...  3.91 us
    pallas_call x1, Pallas kernels, halves(): pl.pallas_call(halves_kernel, grid=(blocks,), in_specs=[spec], out_specs=...  3.86 us
    ppermute x4, starting transfers between devices, exchanged(): return lax.ppermute(x, 'blk', [(i, i ^ 1 << bit) for i in range(count)])  3.04 us
  transfers between devices with their start and end apart: 6, of which 3 were waited for; matrix products, arithmetic and copies ran while one was open for 0% of the time, Pallas kernels for 28%

profile of v1, /device:TPU:0, one launch (start us, length us, event | category | flops | bytes accessed | tf_op | source)
XLA Modules:
  0.0 74.4 jit_solution(9092714099641280138)
XLA Ops:
  0.6 3.9 %halves_and_branch.1 = (bf16[512,1152]{1,0:T(8,128)(2,1)}, s32[1]{0:T(128)}) custom-call(s32[2,8]{1,0:T(2,128)} %grid_ref.1, f32[512,1152]{1,0:T(8,128)} %raw_ref.1), custom_call_target="tpu_custom_call" | custom-call | bytes 4718592 | tf_op jit(solution)/shard_map/halves_and_branch/pallas_call | solution.py:55
  5.2 69.2 %conditional.1 = (f32[512,1152]{1,0:T(8,128)}, f32[512,1152]{1,0:T(8,128)}) conditional(s32[]{:T(128)} %bitcast, (f32[512,1152]{1,0:T(8,128)}, bf16[512,1152]{1,0:T(8,128)(2,1)}, f32[1]{0:T(128)}, f32[1]{0:T(128)}, f32[512,1152]{1,0:T(8,128)}) %tuple.22, (f32[512,1152]{1,0:T(8,128)}, bf16[512,1152]{1,0:T(8,128)(2,1)}, f32[1]{0:T(128)}, ...), branch_computations={%region_0.0_spmd, %region_1.0_spmd, %region_2.0_spmd} | conditional | flops 9663676416 | bytes 89653592 | solution.py:198
  5.2 3.1 %collective-permute-start.8 = (bf16[512,1152]{1,0:T(8,128)(2,1)}, bf16[512,1152]{1,0:T(8,128)(2,1)S(1)}, u32[]{:S(2)}, u32[]{:S(2)}) collective-permute-start(bf16[512,1152]{1,0:T(8,128)(2,1)} %get-tuple-element.44.refs_0_.own_ref), channel_id=1, source_target_pairs={{0,1},{1,2},{2,3},{3,0},{4,5},{5,6},{6,7},{7,4},{8,9},{9,10},{10,1... | collective-permute-start | bytes 3538952 | tf_op jit(solution)/shard_map/cond/branch_1_fun/ppermute | solution.py:163
  8.3 1.5 %collective-permute-start.7 = (bf16[512,1152]{1,0:T(8,128)(2,1)}, bf16[512,1152]{1,0:T(8,128)(2,1)S(1)}, u32[]{:S(2)}, u32[]{:S(2)}) collective-permute-start(bf16[512,1152]{1,0:T(8,128)(2,1)} %get-tuple-element.44.refs_0_.own_ref), channel_id=1, source_target_pairs={{0,16},{4,20},{8,24},{12,28},{16,0},{20,4},{24,8},{28,12},{1,17},{... | collective-permute-start | bytes 3538952 | tf_op jit(solution)/shard_map/cond/branch_1_fun/ppermute | solution.py:168
  9.8 0.0 collective-permute-start.6
  9.8 3.9 %halves.4.own_ref.refs_0_ = bf16[512,1152]{1,0:T(8,128)(2,1)} custom-call(f32[512,1152]{1,0:T(8,128)} %get-tuple-element.81.raw_ref), custom_call_target="tpu_custom_call" | custom-call | bytes 4718592 | tf_op jit(solution)/shard_map/cond/branch_1_fun/halves/pallas_call | solution.py:30
  13.7 1.3 %copy-done.1 = bf16[512,1152]{1,0:T(8,128)(2,1)S(1)} copy-done((bf16[512,1152]{1,0:T(8,128)(2,1)S(1)}, bf16[512,1152]{1,0:T(8,128)(2,1)}, u32[]{:S(2)}) %copy-start.1) | copy-done | bytes 1179672 | tf_op jit(solution)/shard_map/cond
  15.0 4.3 %add_up.9.refs_3_ = f32[512,1152]{1,0:T(8,128)S(1)} custom-call(f32[1]{0:T(128)} %get-tuple-element.84.scale_ref, f32[1]{0:T(128)} %get-tuple-element.87.shift_ref, bf16[512,1152]{1,0:T(8,128)(2,1)} %get-tuple-element.44.refs_0_.own_ref, bf16[512,1152]{1,0:T(8,128)(2,1)S(1)} %copy-done.1), custom_call_target="tpu_custom_call" | custom-call | flops 1207959552 | bytes 4718592 | tf_op jit(solution)/shard_map/cond/branch_1_fun/add_up/pallas_call | solution.py:133
  19.2 0.0 copy-start.4
  19.2 4.4 %add_up.8.refs_3_ = f32[512,1152]{1,0:T(8,128)S(1)} custom-call(f32[1]{0:T(128)} %get-tuple-element.84.scale_ref, f32[1]{0:T(128)} %get-tuple-element.87.shift_ref, bf16[512,1152]{1,0:T(8,128)(2,1)S(1)} %copy-done.1, bf16[512,1152]{1,0:T(8,128)(2,1)} %get-tuple-element.44.refs_0_.own_ref), custom_call_target="tpu_custom_call" | custom-call | flops 1207959552 | bytes 4718592 | tf_op jit(solution)/shard_map/cond/branch_1_fun/add_up/pallas_call | solution.py:133
  23.7 0.0 copy-start.7
  23.7 12.8 %collective-permute-done.8.refs_2_ = bf16[512,1152]{1,0:T(8,128)(2,1)S(1)} collective-permute-done((bf16[512,1152]{1,0:T(8,128)(2,1)}, bf16[512,1152]{1,0:T(8,128)(2,1)S(1)}, u32[]{:S(2)}, u32[]{:S(2)}) %collective-permute-start.8) | collective-permute-done | bytes 1179680 | tf_op jit(solution)/shard_map/cond/branch_1_fun/ppermute | solution.py:163
  36.5 0.0 collective-permute-done.7.refs_1_
  36.5 0.0 collective-permute-done.6.refs_0_
  36.5 1.8 %collective-permute-start.11 = (bf16[512,1152]{1,0:T(8,128)(2,1)S(1)}, bf16[512,1152]{1,0:T(8,128)(2,1)S(1)}, u32[]{:S(2)}, u32[]{:S(2)}) collective-permute-start(bf16[512,1152]{1,0:T(8,128)(2,1)S(1)} %copy-done.1), channel_id=1, source_target_pairs={{0,3},{1,0},{2,1},{3,2},{4,7},{5,4},{6,5},{7,6},{8,11},{9,8},{10,9... | collective-permute-start | bytes 3538952 | tf_op jit(solution)/shard_map/cond/branch_1_fun/ppermute | solution.py:163
  38.3 1.5 %collective-permute-start.10 = (bf16[512,1152]{1,0:T(8,128)(2,1)S(1)}, bf16[512,1152]{1,0:T(8,128)(2,1)S(1)}, u32[]{:S(2)}, u32[]{:S(2)}) collective-permute-start(bf16[512,1152]{1,0:T(8,128)(2,1)S(1)} %copy-done.1), channel_id=1, source_target_pairs={{0,16},{4,20},{8,24},{12,28},{16,0},{20,4},{24,8},{28,12},{1,17},{... | collective-permute-start | bytes 3538952 | tf_op jit(solution)/shard_map/cond/branch_1_fun/ppermute | solution.py:168
  39.8 0.0 collective-permute-start.9
  39.8 0.0 copy-done.4
  39.9 8.2 %finish.8 = f32[512,1152]{1,0:T(8,128)} custom-call(f32[1]{0:T(128)} %get-tuple-element.84.scale_ref, f32[1]{0:T(128)} %get-tuple-element.87.shift_ref, bf16[512,1152]{1,0:T(8,128)(2,1)S(1)} %copy-done.1, f32[512,1152]{1,0:T(8,128)S(1)} %copy-done.4, bf16[512,1152]{1,0:T(8,128)(2,1)S(1)} %collective-permute-done.6.refs_0_, ...), custom_call_target="tpu_custom_call" | custom-call | flops 3623878656 | bytes 11796480 | tf_op jit(solution)/shard_map/cond/branch_1_fun/finish/pallas_call | solution.py:149
  48.1 15.6 %collective-permute-done.11.refs_2_ = bf16[512,1152]{1,0:T(8,128)(2,1)S(1)} collective-permute-done((bf16[512,1152]{1,0:T(8,128)(2,1)S(1)}, bf16[512,1152]{1,0:T(8,128)(2,1)S(1)}, u32[]{:S(2)}, u32[]{:S(2)}) %collective-permute-start.11) | collective-permute-done | bytes 1179680 | tf_op jit(solution)/shard_map/cond/branch_1_fun/ppermute | solution.py:163
  63.7 1.2 %collective-permute-done.10.refs_1_ = bf16[512,1152]{1,0:T(8,128)(2,1)S(1)} collective-permute-done((bf16[512,1152]{1,0:T(8,128)(2,1)S(1)}, bf16[512,1152]{1,0:T(8,128)(2,1)S(1)}, u32[]{:S(2)}, u32[]{:S(2)}) %collective-permute-start.10) | collective-permute-done | bytes 1179680 | tf_op jit(solution)/shard_map/cond/branch_1_fun/ppermute | solution.py:168
  64.9 0.0 collective-permute-done.9.refs_0_
  64.9 0.0 copy-done.7
  64.9 9.5 %finish.9 = f32[512,1152]{1,0:T(8,128)} custom-call(f32[1]{0:T(128)} %get-tuple-element.84.scale_ref, f32[1]{0:T(128)} %get-tuple-element.87.shift_ref, bf16[512,1152]{1,0:T(8,128)(2,1)} %get-tuple-element.44.refs_0_.own_ref, f32[512,1152]{1,0:T(8,128)S(1)} %copy-done.7, bf16[512,1152]{1,0:T(8,128)(2,1)S(1)} %collective-permute-done.9.refs_0_, ...), custom_call_target="tpu_custom_call" | custom-call | flops 3623878656 | bytes 11796480 | tf_op jit(solution)/shard_map/cond/branch_1_fun/finish/pallas_call | solution.py:149
  (1 shorter events, 0.0 us)
Async XLA Ops:
  5.2 31.3 %collective-permute-start.8 = (bf16[512,1152]{1,0:T(8,128)(2,1)}, bf16[512,1152]{1,0:T(8,128)(2,1)S(1)}, u32[]{:S(2)}, u32[]{:S(2)}) collective-permute-start(bf16[512,1152]{1,0:T(8,128)(2,1)} %get-tuple-element.44.refs_0_.own_ref), channel_id=1, source_target_pairs={{0,1},{1,2},{2,3},{3,0},{4,5},{5,6},{6,7},{7,4},{8,9},{9,10},{10,1... | collective-permute-start | bytes 3538952 | tf_op jit(solution)/shard_map/cond/branch_1_fun/ppermute | solution.py:163
  8.3 28.2 %collective-permute-start.7 = (bf16[512,1152]{1,0:T(8,128)(2,1)}, bf16[512,1152]{1,0:T(8,128)(2,1)S(1)}, u32[]{:S(2)}, u32[]{:S(2)}) collective-permute-start(bf16[512,1152]{1,0:T(8,128)(2,1)} %get-tuple-element.44.refs_0_.own_ref), channel_id=1, source_target_pairs={{0,16},{4,20},{8,24},{12,28},{16,0},{20,4},{24,8},{28,12},{1,17},{... | collective-permute-start | bytes 3538952 | tf_op jit(solution)/shard_map/cond/branch_1_fun/ppermute | solution.py:168
  9.8 26.7 %collective-permute-start.6 = (bf16[512,1152]{1,0:T(8,128)(2,1)}, bf16[512,1152]{1,0:T(8,128)(2,1)S(1)}, u32[]{:S(2)}, u32[]{:S(2)}) collective-permute-start(bf16[512,1152]{1,0:T(8,128)(2,1)} %get-tuple-element.44.refs_0_.own_ref), channel_id=1, source_target_pairs={{0,4},{4,0},{8,12},{12,8},{16,20},{20,16},{24,28},{28,24},{1,5},{5... | collective-permute-start | bytes 3538952 | tf_op jit(solution)/shard_map/cond/branch_1_fun/ppermute | solution.py:168
  13.7 1.3 %copy-start.1 = (bf16[512,1152]{1,0:T(8,128)(2,1)S(1)}, bf16[512,1152]{1,0:T(8,128)(2,1)}, u32[]{:S(2)}) copy-start(bf16[512,1152]{1,0:T(8,128)(2,1)} %halves.4.own_ref.refs_0_) | copy-start | bytes 3538948 | tf_op jit(solution)/shard_map/cond
  19.2 20.6 %copy-start.4 = (f32[512,1152]{1,0:T(8,128)S(1)}, f32[512,1152]{1,0:T(8,128)}, u32[]{:S(2)}) copy-start(f32[512,1152]{1,0:T(8,128)} %get-tuple-element.81.raw_ref) | copy-start | bytes 7077892 | tf_op jit(solution)/shard_map/cond
  23.7 41.2 %copy-start.7 = (f32[512,1152]{1,0:T(8,128)S(1)}, f32[512,1152]{1,0:T(8,128)}, u32[]{:S(2)}) copy-start(f32[512,1152]{1,0:T(8,128)} %get-tuple-element.50.raw_ref) | copy-start | bytes 7077892 | tf_op jit(solution)/shard_map/cond
  36.5 27.2 %collective-permute-start.11 = (bf16[512,1152]{1,0:T(8,128)(2,1)S(1)}, bf16[512,1152]{1,0:T(8,128)(2,1)S(1)}, u32[]{:S(2)}, u32[]{:S(2)}) collective-permute-start(bf16[512,1152]{1,0:T(8,128)(2,1)S(1)} %copy-done.1), channel_id=1, source_target_pairs={{0,3},{1,0},{2,1},{3,2},{4,7},{5,4},{6,5},{7,6},{8,11},{9,8},{10,9... | collective-permute-start | bytes 3538952 | tf_op jit(solution)/shard_map/cond/branch_1_fun/ppermute | solution.py:163
  38.3 26.6 %collective-permute-start.10 = (bf16[512,1152]{1,0:T(8,128)(2,1)S(1)}, bf16[512,1152]{1,0:T(8,128)(2,1)S(1)}, u32[]{:S(2)}, u32[]{:S(2)}) collective-permute-start(bf16[512,1152]{1,0:T(8,128)(2,1)S(1)} %copy-done.1), channel_id=1, source_target_pairs={{0,16},{4,20},{8,24},{12,28},{16,0},{20,4},{24,8},{28,12},{1,17},{... | collective-permute-start | bytes 3538952 | tf_op jit(solution)/shard_map/cond/branch_1_fun/ppermute | solution.py:168
  39.8 25.0 %collective-permute-start.9 = (bf16[512,1152]{1,0:T(8,128)(2,1)S(1)}, bf16[512,1152]{1,0:T(8,128)(2,1)S(1)}, u32[]{:S(2)}, u32[]{:S(2)}) collective-permute-start(bf16[512,1152]{1,0:T(8,128)(2,1)S(1)} %copy-done.1), channel_id=1, source_target_pairs={{0,4},{4,0},{8,12},{12,8},{16,20},{20,16},{24,28},{28,24},{1,5},{5... | collective-permute-start | bytes 3538952 | tf_op jit(solution)/shard_map/cond/branch_1_fun/ppermute | solution.py:168
